TPU v7x, 256 devices: a whole 4x4x8 slice. The times are simulated.
256 devices in a mesh: list: 64 (over y, z, core), sub: 4 (over x).
Axes of the slice: x: 4, y: 4, z: 8, core: 2. Of those that a mesh axis runs over, the one named last changes fastest.
Arguments:
- embeddings: bfloat16 [65536, 1280], P(('list', 'sub')), may hold values from -54 to 54
- coarse_list_index: int32 [65536], P(('list', 'sub')), may hold values from 0 to 65535, as said below
- slots: int32 [65536], P(('list', 'sub')), may hold values from 0 to 7, as said below
- codes: int32 [65536, 128], P(('list', 'sub')), may hold values from 0 to 255
- centroids: bfloat16 [65536, 1280], P('list'), may hold values from -6 to 6
- rotation: bfloat16 [1280, 1280], P(None, 'sub'), may hold values from -0.15625 to 0.15625
- old_codebook: float32 [256, 1280], P('list', 'sub'), may hold values from -6 to 6
Outputs:
- list_store: bfloat16 [131072, 1280], P('list', 'sub')
- codebook: float32 [256, 1280], P('list', 'sub')
Inputs may be any that keep to these rules, and one draw needn't show every extreme that they name: `coarse_list_index`: the owner of list i is i // 1024. Rows of one device with the same owner have distinct slots; for a quarter of the owners every device fills all 8 slots.
All inputs are finite; a program needn't handle non-finite values.
Results may differ from a plain program's by a relative error of at most 0.005.
Values may be sent and summed in bfloat16 or wider, within the bound.
A program may use at most 64 MiB of HBM per device.

v0:
```python
import math

import jax
import jax.numpy as jnp
from jax import lax
from jax.sharding import PartitionSpec as P

CENT = 256
LIST_DEV = 1024


def code_tables(rotated, local_code_assignments, dsub):
    total_rows = local_code_assignments.shape[0]
    subs_dev = local_code_assignments.shape[1]
    per_step = math.gcd(subs_dev, 4)
    steps_count = subs_dev // per_step
    values_blocks = rotated.reshape(total_rows, steps_count, per_step, dsub).transpose(1, 0, 2, 3)
    code_blocks = local_code_assignments.reshape(total_rows, steps_count, per_step).transpose(
        1, 0, 2
    )
    entries_all = jnp.arange(CENT, dtype=jnp.int32)

    def single_update_step(carry, pieces):
        residual_value_slice, code_piece = pieces
        indicator_matrix = (code_piece[:, :, None] == entries_all[None, None, :]).astype(
            jnp.bfloat16
        )
        part_sums = jnp.einsum(
            "hme,hmc->mec",
            indicator_matrix,
            residual_value_slice,
            preferred_element_type=jnp.float32,
        )
        part_counts = jnp.sum(indicator_matrix, axis=0, dtype=jnp.float32)
        return (carry, (part_sums, part_counts))

    unused, (sum_blocks, count_blocks) = lax.scan(
        single_update_step, 0, (values_blocks, code_blocks)
    )
    sums = (
        sum_blocks.reshape(subs_dev, CENT, dsub).transpose(1, 0, 2).reshape(CENT, subs_dev * dsub)
    )
    counts = count_blocks.reshape(subs_dev, CENT).T
    return (sums, counts)


def shards(embeddings, coarse_list_index, slots, codes, centroids, rotation, old_codebook):
    owners = lax.axis_size("list")
    groups = lax.axis_size("sub")
    row_dev = embeddings.shape[0]
    width = embeddings.shape[1]
    subs_all = codes.shape[1]
    capacity = 2 * row_dev // owners
    target_vectors = coarse_list_index // LIST_DEV * capacity + slots
    outbound = (
        jnp.zeros((owners * capacity, width), jnp.bfloat16).at[target_vectors].set(embeddings)
    )
    outbound = outbound.reshape(owners, capacity, width)
    code_out = jnp.full((owners * capacity, subs_all), -1, jnp.int32).at[target_vectors].set(codes)
    code_out = code_out.reshape(owners, capacity, subs_all)
    local_out = (
        jnp.full((owners * capacity,), -1, jnp.int32)
        .at[target_vectors]
        .set(coarse_list_index % LIST_DEV)
    )
    local_out = local_out.reshape(owners, capacity)
    arrived = lax.all_to_all(outbound, "list", split_axis=0, concat_axis=0, tiled=True).reshape(
        owners * capacity, width
    )
    code_in, local_in = (
        lax.all_to_all(code_out, "list", split_axis=0, concat_axis=0, tiled=True),
        lax.all_to_all(local_out, "list", split_axis=0, concat_axis=0, tiled=True),
    )
    code_in = code_in.reshape(owners * capacity, subs_all)
    local_in = local_in.reshape(owners * capacity)
    filled = local_in >= 0
    centroid_row_vectors = jnp.take(centroids, jnp.maximum(local_in, 0), axis=0)
    residual = jnp.where(
        filled[:, None], arrived.astype(jnp.float32) - centroid_row_vectors.astype(jnp.float32), 0.0
    ).astype(jnp.bfloat16)
    rotated = jnp.dot(
        lax.all_gather(residual, "sub", axis=0, tiled=True),
        rotation,
        preferred_element_type=jnp.float32,
    ).astype(jnp.bfloat16)
    local_code_assignments = lax.all_to_all(code_in, "sub", split_axis=1, concat_axis=0, tiled=True)
    subs_dev = local_code_assignments.shape[1]
    dsub = rotated.shape[1] // subs_dev
    sums, counts = code_tables(rotated, local_code_assignments, dsub)
    entries = CENT // owners
    total_sums, total_counts = lax.psum((sums, counts), "list")
    first = lax.axis_index("list") * entries
    my_sums = lax.dynamic_slice_in_dim(total_sums, first, entries, 0)
    my_counts = lax.dynamic_slice_in_dim(total_counts, first, entries, 0)
    anchor_weight = row_dev * owners * groups // (4 * CENT)
    expanded = jnp.repeat(my_counts, dsub, axis=1)
    codebook = (my_sums + anchor_weight * old_codebook) / (expanded + anchor_weight)
    return (rotated, codebook)


def solution(mesh):
    return jax.shard_map(
        shards,
        mesh=mesh,
        in_specs=(
            P(("list", "sub"), None),
            P(("list", "sub")),
            P(("list", "sub")),
            P(("list", "sub"), None),
            P("list", None),
            P(None, "sub"),
            P("list", "sub"),
        ),
        out_specs=(P("list", "sub"), P("list", "sub")),
        check_vma=False,
    )
```

profile of v0, /device:TPU:1, one launch (start us, length us, event | category | flops | bytes accessed | tf_op | source)
XLA Modules:
  0.0 446.5 jit_solution(16686279295250189324)
XLA Ops:
  7.2 0.9 and_select_fusion
  8.0 1.4 scatter_custom_fusion
  9.4 0.7 all_to_all.24
  10.1 13.2 %all-to-all-start = ((s32[64,1,8]{2,1,0:T(1,128)}), s32[64,1,8]{2,1,0:T(1,128)S(1)}, u32[]{:S(2)}, u32[]{:S(2)}) async-start(s32[64,1,8]{2,1,0:T(1,128)} %bitcast), calls=%async_computation | async-start | bytes 65536 | tf_op jit(solution)/shard_map/all_to_all | solution.py:72
  23.3 3.5 scatter_custom_fusion.1
  26.8 5.8 %all-to-all-done = s32[64,1,8]{2,1,0:T(1,128)S(1)} async-done(((s32[64,1,8]{2,1,0:T(1,128)}), s32[64,1,8]{2,1,0:T(1,128)S(1)}, u32[]{:S(2)}, u32[]{:S(2)}) %all-to-all-start) | async-done | bytes 2080 | tf_op jit(solution)/shard_map/all_to_all | solution.py:72
  32.6 5.5 %all-to-all-start.1 = ((bf16[64,8,1280]{2,1,0:T(8,128)(2,1)}), bf16[64,8,1280]{2,1,0:T(8,128)(2,1)}, u32[]{:S(2)}, u32[]{:S(2)}) async-start(bf16[64,8,1280]{2,1,0:T(8,128)(2,1)} %bitcast.40), calls=%async_computation.1 | async-start | bytes 2621440 | tf_op jit(solution)/shard_map/all_to_all | solution.py:67
  38.2 0.2 compare_reduce_fusion.1
  38.4 0.1 ge.18
  38.5 0.1 le.16
  38.6 0.1 maximum_reduce_fusion
  38.7 0.1 reshape.87
  38.8 2.9 gather_fusion
  41.7 30.6 %all-to-all-done.1 = bf16[64,8,1280]{2,1,0:T(8,128)(2,1)} async-done(((bf16[64,8,1280]{2,1,0:T(8,128)(2,1)}), bf16[64,8,1280]{2,1,0:T(8,128)(2,1)}, u32[]{:S(2)}, u32[]{:S(2)}) %all-to-all-start.1) | async-done | bytes 1310752 | tf_op jit(solution)/shard_map/all_to_all | solution.py:67
  72.2 3.3 fusion.11
  75.6 1.6 scatter_custom_fusion.2
  77.2 18.1 %all_to_all.35 = s32[64,8,128]{2,1,0:T(8,128)S(1)} all-to-all(s32[64,8,128]{2,1,0:T(8,128)S(1)} %bitcast.43), channel_id=1, replica_groups=mesh['list'=64,'sub'=4] {'list'}, dimensions={0} | all-to-all | bytes 524288 | tf_op jit(solution)/shard_map/all_to_all | solution.py:71
  95.2 1.5 all_to_all.28
  96.7 2.2 copy.36
  98.9 4.0 all-to-all-start.3
  103.0 9.6 %all-to-all-done.3 = s32[512,4,32]{0,2,1:T(8,128)S(1)} async-done(((s32[512,4,32]{0,2,1:T(8,128)}), s32[512,4,32]{0,2,1:T(8,128)S(1)}, u32[]{:S(2)}, u32[]{:S(2)}) %all-to-all-start.3) | async-done | bytes 262176 | tf_op jit(solution)/shard_map/all_to_all | solution.py:86
  112.6 0.2 copy.37
  112.7 0.2 reshape.79
  113.0 22.0 %all-gather.2.cloned.1.call-done = bf16[2048,1280]{1,0:T(8,128)(2,1)} async-done(((bf16[512,1280]{1,0:T(8,128)(2,1)}), bf16[2048,1280]{1,0:T(8,128)(2,1)}) %all-gather.2.cloned.1.call-update) | async-done | bytes 5242896 | tf_op jit(solution)/shard_map/all_gather | solution.py:82
  134.9 5.6 %convolution_convert_fusion = bf16[2048,320]{0,1:T(8,128)(2,1)} fusion(bf16[2048,1280]{1,0:T(8,128)(2,1)} %all-gather.2.cloned.1.call-done, bf16[1280,320]{0,1:T(8,128)(2,1)} %param.14), kind=kOutput, calls=%fused_computation.17 | convolution fusion | flops 1678376960 | bytes 7372800 | tf_op jit(solution)/shard_map/dot_general | solution.py:81
  140.6 3.4 reshape.80
  144.0 46.9 %while.13 = (s32[]{:T(128)}, f32[8,4,256,10]{2,3,1,0:T(8,128)S(1)}, f32[8,4,256]{2,1,0:T(4,128)S(1)}, s32[8,2048,4]{1,2,0:T(4,128)S(1)}, bf16[8,2048,4,10]{1,3,2,0:T(8,128)(2,1)}, /*index=5*/s32[]{:T(128)}) while((s32[]{:T(128)}, f32[8,4,256,10]{2,3,1,0:T(8,128)S(1)}, f32[8,4,256]{2,1,0:T(4,128)S(1)}, s32[8,2048,4]{1,2,0:T(4,128)S(1)}, ...), condition=%wide.region_5.6_spmd.clone, body=%wide.region_3.5_spmd.clone.sunk | while | flops 52427776 | bytes 472141 | solution.py:37
  144.0 3.2 fusion.23
  147.2 2.6 convert_reduce_fusion.2
  149.9 3.2 fusion.23
  153.0 2.6 convert_reduce_fusion.2
  155.7 3.2 fusion.23
  158.9 2.6 convert_reduce_fusion.2
  161.6 3.2 fusion.23
  164.8 2.6 convert_reduce_fusion.2
  167.4 3.2 fusion.23
  170.6 2.6 convert_reduce_fusion.2
  173.3 3.2 fusion.23
  176.5 2.6 convert_reduce_fusion.2
  179.2 3.2 fusion.23
  182.4 2.6 convert_reduce_fusion.2
  185.0 3.2 fusion.23
  188.2 2.6 convert_reduce_fusion.2
  190.9 0.9 copy.38
  191.9 0.1 copy.39
  192.0 246.1 %psum.15 = f32[256,32]{1,0:T(8,128)S(1)} all-reduce(f32[256,32]{1,0:T(8,128)S(1)} %bitcast.45), channel_id=1, replica_groups=mesh['list'=64,'sub'=4] {'list'}, use_global_device_ids=true, to_apply=%region_7.8 | all-reduce | flops 8192 | bytes 65536 | tf_op jit(solution)/shard_map/psum | solution.py:91
  438.2 0.1 add.46
  438.4 1.3 add_divide_fusion
  (34 shorter events, 0.4 us)
Async XLA Ops:
  7.2 31.6 %copy-start = (bf16[1024,1280]{1,0:T(8,128)(2,1)S(1)}, bf16[1024,1280]{1,0:T(8,128)(2,1)}, u32[]{:S(2)}) copy-start(bf16[1024,1280]{1,0:T(8,128)(2,1)} %param.13) | copy-start | bytes 7864324
  10.1 22.4 %all-to-all-start = ((s32[64,1,8]{2,1,0:T(1,128)}), s32[64,1,8]{2,1,0:T(1,128)S(1)}, u32[]{:S(2)}, u32[]{:S(2)}) async-start(s32[64,1,8]{2,1,0:T(1,128)} %bitcast), calls=%async_computation | async-start | bytes 65536 | tf_op jit(solution)/shard_map/all_to_all | solution.py:72
  32.6 39.7 %all-to-all-start.1 = ((bf16[64,8,1280]{2,1,0:T(8,128)(2,1)}), bf16[64,8,1280]{2,1,0:T(8,128)(2,1)}, u32[]{:S(2)}, u32[]{:S(2)}) async-start(bf16[64,8,1280]{2,1,0:T(8,128)(2,1)} %bitcast.40), calls=%async_computation.1 | async-start | bytes 2621440 | tf_op jit(solution)/shard_map/all_to_all | solution.py:67
  38.1 96.8 %all-gather.2.cloned.1.call-start = ((), (), s32[]{:S(2)}) async-start(), calls=%async_computation.4 | async-start | bytes 6553600 | tf_op jit(solution)/shard_map/all_gather | solution.py:82
  98.9 13.6 %all-to-all-start.3 = ((s32[512,4,32]{0,2,1:T(8,128)}), s32[512,4,32]{0,2,1:T(8,128)S(1)}, u32[]{:S(2)}, u32[]{:S(2)}) async-start(s32[512,4,32]{0,2,1:T(8,128)} %copy.36), calls=%async_computation.3 | async-start | bytes 524288 | tf_op jit(solution)/shard_map/all_to_all | solution.py:86
  103.0 335.4 %all-reduce.2.cloned.1.call-start = ((), (), s32[]{:S(2)}) async-start(), calls=%async_computation.5 | async-start | bytes 786432 | tf_op jit(solution)/shard_map/psum | solution.py:91
  140.6 3.4 copy-start.1
  190.9 247.5 %copy-start.2 = (f32[4,320]{1,0:T(4,128)S(1)}, f32[4,320]{1,0:T(4,128)}, u32[]{:S(2)}) copy-start(f32[4,320]{1,0:T(4,128)} %param.15) | copy-start | bytes 15364
Sparse Core Ops, SparseCore 0:
  75.7 59.1 all-gather.1
  192.0 179.3 all-reduce.1
where the time goes:
time: 452 us; the launch traced here: 447 us
  blocking collectives  264 us (58%)
  waiting for transfers between devices  68 us (15%)
  matrix products  31.2 us (7%)
  other arithmetic  26.8 us (6%)
  starting transfers between devices  22.7 us (5%)
  local copies, waits for them, and re-layouts  19.2 us (4%)
  between operations  14.2 us (3%)
    psum x1, blocking collectives, shards(): total_sums, total_counts = lax.psum((sums, counts), 'list')  246 us
    all_to_all x1, waiting for transfers between devices, shards(): lax.all_to_all(outbound, 'list', split_axis=0, concat_axis=0, tiled=True)  30.6 us
    dot_general x8, matrix products, single_update_step(): jnp.einsum('hme,hmc->mec', indicator_matrix, residual_value_slice, prefer...  25.5 us
    all_gather x1, waiting for transfers between devices, shards(): lax.all_gather(residual, 'sub', axis=0, tiled=True)  22 us
    reduce_sum x8, other arithmetic, single_update_step(): part_counts = jnp.sum(indicator_matrix, axis=0, dtype=jnp.float32)  21 us
    all_to_all x1, blocking collectives, shards(): lax.all_to_all(code_out, 'list', split_axis=0, concat_axis=0, tiled=True)  18.1 us
    all_to_all x1, starting transfers between devices, shards(): lax.all_to_all(local_out, 'list', split_axis=0, concat_axis=0, tiled=True)  13.2 us
    all_to_all x1, waiting for transfers between devices, shards(): lax.all_to_all(code_in, 'sub', split_axis=1, concat_axis=0, tiled=True)  9.6 us
  transfers between devices with their start and end apart: 5, of which 4 were waited for; matrix products, arithmetic and copies ran while one was open for 3% of the time, Pallas kernels for 0%

commit v1 on v0

v1 whole, which is shorter than its diff:
```python
import functools

import jax
import jax.numpy as jnp
import numpy as np
from jax import lax
from jax.experimental import pallas as pl
from jax.experimental.pallas import tpu as pltpu
from jax.sharding import PartitionSpec as P

MESH = pl.DeviceIdType.MESH
NY, NZ, NC, NX = 4, 8, 2, 4
OWNERS = NY * NZ * NC
ROW_DEV = 256
CAP = 8
D = 1280
HALF = D // 2
COLS = D // NX
CENT = 256
LIST_DEV = 1024
SUBS_DEV = 32
DSUB = 10
GROUPS = 4
CHIPS_G = 8
CHIPS = NY * NZ
ROWS_G = CHIPS_G * NC * CAP
MW = D + 256
PW = 384
PAY = COLS + SUBS_DEV
NT = (((1,), (1,)), ((), ()))
LANES = 128
SPLIT = (11, 11, 10)
FIRST = (0, 11, 22)
ANCHOR = 64.0
BF = jnp.bfloat16
F32 = jnp.float32


def layout_tables():
    spread = np.zeros((2 * PW, PAY), np.float32)
    back = np.zeros((2, len(SPLIT), LANES, COLS), np.float32)
    for g, (first, many) in enumerate(zip(FIRST, SPLIT)):
        for i in range(many):
            m = first + i
            for d in range(DSUB + 1):
                lane = i * (DSUB + 1) + d
                spread[PW + g * LANES + lane, COLS + m] = 1
                if d < DSUB:
                    spread[g * LANES + lane, m * DSUB + d] = 1
                    back[0, g, lane, m * DSUB + d] = 1
                    back[1, g, i * (DSUB + 1) + DSUB, m * DSUB + d] = 1
    return spread, back


def kernel(
    emb_hbm,
    idx_hbm,
    slot_hbm,
    codes_hbm,
    cent_hbm,
    rot_hbm,
    old_hbm,
    spread_hbm,
    back_hbm,
    store_hbm,
    book_ref,
    emb,
    idx,
    slot,
    codes,
    cent,
    rot,
    old,
    spread,
    back,
    outb,
    inb,
    res,
    pay_out,
    pay_in,
    hot,
    vals,
    acc,
    sum_out,
    sum_pair,
    sum_mid,
    sum_in,
    load_sem,
    swap_send,
    swap_recv,
    out_sem,
    in_sem,
    rot_send,
    rot_recv,
    pay_send,
    pay_recv,
    own_sem,
    pair_send,
    pair_recv,
    sum_send,
    sum_recv,
    store_sem,
):
    me = lax.axis_index("list")
    x = lax.axis_index("sub")
    core = lax.rem(me, NC)
    chip = me // NC
    z = lax.rem(chip, NZ)
    y = chip // NZ
    sibling = me + 1 - 2 * core
    right, left = lax.rem(x + 1, NX), lax.rem(x + NX - 1, NX)
    across = lax.rem(x + 2, NX)

    sources = [(emb_hbm, emb), (idx_hbm, idx), (slot_hbm, slot), (codes_hbm, codes)]
    loads = [
        pltpu.make_async_copy(src, dst.at[core], load_sem.at[i])
        for i, (src, dst) in enumerate(sources)
    ]
    later = [(cent_hbm, cent), (rot_hbm, rot.at[x]), (spread_hbm, spread), (back_hbm, back)]
    later.append((old_hbm, old))
    loads += [
        pltpu.make_async_copy(src, dst, load_sem.at[4 + i]) for i, (src, dst) in enumerate(later)
    ]
    for load in loads:
        load.start()

    barrier = pltpu.get_barrier_semaphore()

    def peer_of(k):
        return lax.rem(chip + k, CHIPS) * NC + core

    def greet(k, carry):
        pl.semaphore_signal(barrier, inc=1, device_id=(peer_of(k), x), device_id_type=MESH)
        return carry

    lax.fori_loop(1, CHIPS, greet, 0)
    pl.semaphore_signal(barrier, inc=1, device_id=(sibling, x), device_id_type=MESH)
    for k in range(1, NX):
        pl.semaphore_signal(
            barrier, inc=1, device_id=(me, lax.rem(x + k, NX)), device_id_type=MESH
        )
    pl.semaphore_wait(barrier, CHIPS + NX - 1)

    swaps = [
        pltpu.make_async_remote_copy(
            src_ref=src,
            dst_ref=dst.at[core],
            send_sem=swap_send.at[i],
            recv_sem=swap_recv.at[i],
            device_id=(sibling, x),
            device_id_type=MESH,
        )
        for i, (src, dst) in enumerate(sources)
    ]
    for swap in swaps:
        swap.start()

    half = COLS // 2
    half_rows = pl.ds(pl.multiple_of(core * half, half), half)
    quarter_a = pl.ds(pl.multiple_of(core * half, half // 2), half // 2)
    quarter_b = pl.ds(pl.multiple_of(core * half + half // 2, half // 2), half // 2)

    def rot_copy(src, block, rows, number, l, s):
        return pltpu.make_async_remote_copy(
            src_ref=src,
            dst_ref=rot.at[block, rows, :],
            send_sem=rot_send.at[number],
            recv_sem=rot_recv.at[number],
            device_id=(l, s),
            device_id_type=MESH,
        )

    to_right = rot_copy(rot_hbm.at[half_rows, :], x, half_rows, 0, me, right)
    to_left = rot_copy(rot_hbm.at[half_rows, :], x, half_rows, 1, me, left)
    to_right.start()
    to_left.start()

    for load in loads[:4]:
        load.wait()
    for swap in swaps:
        swap.wait_recv()
    row_iota = lax.broadcasted_iota(jnp.int32, (ROWS_G, 1), 0)
    lane_iota = lax.broadcasted_iota(jnp.int32, (1, LANES), 1)

    def row_copy(g, j, l):
        return pltpu.make_async_remote_copy(
            src_ref=outb.at[g, j],
            dst_ref=inb.at[g, z],
            send_sem=out_sem.at[g],
            recv_sem=in_sem.at[g],
            device_id=(l, x),
            device_id_type=MESH,
        )

    def send_group(g, carry):
        to_y = lax.rem(y + g, NY)
        to_z = lax.rem(z + row_iota // (NC * CAP), NZ)
        wanted = (to_y * NZ + to_z) * (NC * CAP) + lax.rem(row_iota, NC * CAP)
        made = jnp.zeros((ROWS_G, D), F32)
        code_tile = jnp.zeros((ROWS_G, LANES), F32)
        ids = jnp.zeros((ROWS_G, 1), F32)
        for c in range(NC):
            list_id = idx[c]
            owner = list_id // LIST_DEV
            target = (owner // NC * NC + c) * CAP + slot[c]
            match = (wanted == target) & (lax.rem(owner, NC) == core)
            place = jnp.where(match, 1.0, 0.0).astype(BF)
            local = lax.rem(list_id, LIST_DEV).astype(F32) + 4.0
            ids += jnp.sum(jnp.where(match, local, 0.0), axis=1, keepdims=True)
            code_tile += jnp.dot(
                place, (codes[c] + 1).astype(F32).astype(BF), preferred_element_type=F32
            )
            made += jnp.dot(place, emb[c], preferred_element_type=F32)
        id_int = ids.astype(jnp.int32)
        ids_tile = jnp.where(
            lane_iota < LANES // 2, (id_int // 4).astype(F32), lax.rem(id_int, 4).astype(F32)
        )
        outb[g, :, :, 0:D] = made.astype(BF).reshape(CHIPS_G, NC * CAP, D)
        outb[g, :, :, D : D + LANES] = code_tile.astype(BF).reshape(CHIPS_G, NC * CAP, LANES)
        outb[g, :, :, D + LANES : MW] = ids_tile.astype(BF).reshape(CHIPS_G, NC * CAP, LANES)

        def send(j, carry):
            row_copy(g, j, (to_y * NZ + lax.rem(z + j, NZ)) * NC + core).start()
            return carry

        lax.fori_loop(jnp.where(g == 0, 1, 0), CHIPS_G, send, 0)
        return carry

    lax.fori_loop(0, GROUPS, send_group, 0)
    own_block = pltpu.make_async_copy(outb.at[0, 0], inb.at[0, z], own_sem.at[0])
    own_block.start()

    def to_sibling(block, number):
        copy = rot_copy(rot.at[block, half_rows, :], block, half_rows, number, sibling, x)
        copy.start()
        return copy

    to_right.wait_recv()
    on_right = rot_copy(rot.at[left, quarter_a, :], left, quarter_a, 2, me, right)
    on_right.start()
    to_left.wait_recv()
    on_left = rot_copy(rot.at[right, quarter_b, :], right, quarter_b, 3, me, left)
    on_left.start()
    shared = [to_sibling(left, 4), to_sibling(right, 5)]
    on_right.wait_recv()
    on_left.wait_recv()
    shared.append(to_sibling(across, 6))
    for load in loads[4:]:
        load.wait()
    own_block.wait()
    for copy in shared:
        copy.wait_recv()

    list_iota = lax.broadcasted_iota(jnp.int32, (1, LIST_DEV), 1)
    row_of_sums = lax.broadcasted_iota(jnp.int32, (1, OWNERS, 1), 1)
    entry_iota = lax.rem(row_of_sums, CHIPS) * NC + row_of_sums // CHIPS
    sum_row = lax.broadcasted_iota(jnp.int32, (LANES, 1), 0)
    is_count = lax.rem(sum_row, DSUB + 1) == DSUB
    same = lax.broadcasted_iota(jnp.int32, (LANES, LANES), 0) == lax.broadcasted_iota(
        jnp.int32, (LANES, LANES), 1
    )
    unit = jnp.where(same, 1.0, 0.0).astype(BF)

    def group_copy(g, many):
        return pltpu.make_async_remote_copy(
            src_ref=outb.at[g, 0:many],
            dst_ref=inb.at[g, 0:many],
            send_sem=out_sem.at[g],
            recv_sem=in_sem.at[g],
            device_id=(sibling, x),
            device_id_type=MESH,
        )

    def pay_copy(g, dt):
        to = lax.rem(x + dt, NX)
        return pltpu.make_async_remote_copy(
            src_ref=pay_out.at[g, to],
            dst_ref=pay_in.at[g, :, pl.ds(pl.multiple_of(x * ROWS_G, ROWS_G), ROWS_G)],
            send_sem=pay_send.at[g, dt],
            recv_sem=pay_recv.at[g, dt],
            device_id=(me, to),
            device_id_type=MESH,
        )

    def store_copy(g, s):
        from_y = lax.rem(y - g + NY, NY)
        to = pl.multiple_of(s * (OWNERS * CAP) + from_y * ROWS_G, ROWS_G)
        return pltpu.make_async_copy(
            pay_in.at[g, 0:COLS, s * ROWS_G : (s + 1) * ROWS_G],
            store_hbm.at[:, pl.ds(to, ROWS_G)],
            store_sem.at[g, s],
        )

    def rotate_group(g):
        @pl.when(g == 0)
        def _():
            group_copy(0, CHIPS_G - 1).wait_recv()

        @pl.when(g > 0)
        def _():
            group_copy(g, CHIPS_G).wait_recv()

        ids_tile = inb[g, :, :, D + LANES : MW].astype(F32).reshape(ROWS_G, LANES)
        list_row = (
            ids_tile[:, 0:1] * 4.0 + ids_tile[:, LANES // 2 : LANES // 2 + 1] - 4.0
        ).astype(jnp.int32)
        chosen = jnp.where(list_row == list_iota, 1.0, 0.0).astype(BF)
        for part in range(2):
            cut = slice(part * HALF, (part + 1) * HALF)
            picked = jnp.dot(chosen, cent[:, cut], preferred_element_type=F32)
            rows = inb[g, :, :, cut].astype(F32).reshape(ROWS_G, HALF)
            res[:, cut] = (rows - picked).astype(BF)
        code_tile = inb[g, :, :, D : D + LANES].reshape(ROWS_G, LANES)
        code_rows = lax.dot_general(unit, code_tile, NT, preferred_element_type=F32).astype(BF)
        for t in range(NX):
            turned = lax.dot_general(rot[t], res[...], NT, preferred_element_type=F32)
            pay_out[g, t, 0:COLS, :] = turned.astype(BF)
            pay_out[g, t, COLS:PAY, :] = code_rows[t * SUBS_DEV : (t + 1) * SUBS_DEV, :]
        for dt in (2, 1, 3):
            pay_copy(g, dt).start()
        own = pl.ds(pl.multiple_of(x * ROWS_G, ROWS_G), ROWS_G)
        pay_in[g, :, own] = pay_out[g, x]

    def count_group(g):
        for dt in range(1, NX):
            pay_copy(g, dt).wait_recv()
        for s in range(NX):
            store_copy(g, s).start()
        upper = (pay_in[g, COLS:PAY, :].astype(F32).astype(jnp.int32) - 1) >> 2
        for part, (first, many) in enumerate(zip(FIRST, SPLIT)):
            value = jnp.dot(
                spread[part * LANES : (part + 1) * LANES, :], pay_in[g], preferred_element_type=F32
            )
            value = jnp.where(is_count, 1.0, value)
            lower = jnp.dot(
                spread[PW + part * LANES : PW + (part + 1) * LANES, :],
                pay_in[g],
                preferred_element_type=F32,
            )
            lower = (lower.astype(jnp.int32) - 1) & 3
            for lo in range(4):
                vals[lo * LANES : (lo + 1) * LANES, :] = jnp.where(lower == lo, value, 0.0).astype(
                    BF
                )
            ones = jnp.where(upper[first : first + many][:, None, :] == entry_iota, 1.0, 0.0)
            hot[0 : many * OWNERS, :] = ones.astype(BF).reshape(many * OWNERS, NX * ROWS_G)
            acc[part, 0 : many * OWNERS, :] += lax.dot_general(
                hot[0 : many * OWNERS, :], vals[...], NT, preferred_element_type=F32
            )

    acc[...] = jnp.zeros_like(acc)

    def both(g, carry):
        @pl.when(g < GROUPS)
        def _():
            rotate_group(g)

        @pl.when(g > 0)
        def _():
            count_group(g - 1)

        return carry

    lax.fori_loop(0, GROUPS + 1, both, 0)

    subspace = lane_iota // (DSUB + 1)
    for part, many in enumerate(SPLIT):
        for lo in range(4):
            cut = slice(lo * LANES, (lo + 1) * LANES)
            total = jnp.zeros((OWNERS, LANES), F32)
            for i in range(many):
                total = jnp.where(
                    subspace == i, acc[part, i * OWNERS : (i + 1) * OWNERS, cut], total
                )
            sum_out[:, :, part * 4 + lo, :] = total.reshape(NC, CHIPS, LANES)

    pair = pltpu.make_async_remote_copy(
        src_ref=sum_out.at[1 - core],
        dst_ref=sum_pair,
        send_sem=pair_send,
        recv_sem=pair_recv,
        device_id=(sibling, x),
        device_id_type=MESH,
    )
    pair.start()
    pair.wait_recv()
    sum_mid[...] = sum_out[core] + sum_pair[...]

    def send_sum(k, carry):
        pltpu.make_async_remote_copy(
            src_ref=sum_mid.at[lax.rem(chip + k, CHIPS)],
            dst_ref=sum_in.at[k],
            send_sem=sum_send,
            recv_sem=sum_recv,
            device_id=(peer_of(k), x),
            device_id_type=MESH,
        ).start()
        return carry

    lax.fori_loop(1, CHIPS, send_sum, 0)
    sum_in[0] = sum_mid[chip]
    all_sums = pltpu.make_async_remote_copy(
        src_ref=sum_mid.at[1:CHIPS],
        dst_ref=sum_in.at[1:CHIPS],
        send_sem=sum_send,
        recv_sem=sum_recv,
        device_id=(sibling, x),
        device_id_type=MESH,
    )
    all_sums.wait_recv()
    total = jnp.sum(sum_in[...], axis=0)
    sums = jnp.zeros((4, COLS), F32)
    counts = jnp.zeros((4, COLS), F32)
    for part in range(len(SPLIT)):
        tile = total[part * 4 : part * 4 + 4, :]
        sums += jnp.dot(
            tile, back[0, part], preferred_element_type=F32, precision=lax.Precision.HIGHEST
        )
        counts += jnp.dot(
            tile, back[1, part], preferred_element_type=F32, precision=lax.Precision.HIGHEST
        )
    book_ref[...] = (sums + ANCHOR * old[...]) / (counts + ANCHOR)

    for swap in swaps:
        swap.wait_send()
    group_copy(0, CHIPS_G - 1).wait_send()
    for g in range(1, GROUPS):
        group_copy(g, CHIPS_G).wait_send()
    for copy in [to_right, to_left, on_right, on_left] + shared:
        copy.wait_send()
    for g in range(GROUPS):
        for dt in range(1, NX):
            pay_copy(g, dt).wait_send()
    pair.wait_send()
    all_sums.wait_send()
    for g in range(GROUPS):
        for s in range(NX):
            store_copy(g, s).wait()


def shards(embeddings, coarse_list_index, slots, codes, centroids, rotation, old_codebook):
    spread, back = layout_tables()
    vmem = pl.BlockSpec(memory_space=pltpu.VMEM)
    anywhere = pl.BlockSpec(memory_space=pl.ANY)
    dma = pltpu.SemaphoreType.DMA
    store, book = pl.pallas_call(
        kernel,
        out_shape=(
            jax.ShapeDtypeStruct((COLS, OWNERS * NX * CAP), BF),
            jax.ShapeDtypeStruct((CENT // OWNERS, COLS), F32),
        ),
        in_specs=[anywhere] * 9,
        out_specs=(anywhere, vmem),
        scratch_shapes=[
            pltpu.VMEM((NC, ROW_DEV, D), BF),
            pltpu.VMEM((NC, 1, ROW_DEV), jnp.int32),
            pltpu.VMEM((NC, 1, ROW_DEV), jnp.int32),
            pltpu.VMEM((NC, ROW_DEV, LANES), jnp.int32),
            pltpu.VMEM((LIST_DEV, D), BF),
            pltpu.VMEM((NX, COLS, D), BF),
            pltpu.VMEM((CENT // OWNERS, COLS), F32),
            pltpu.VMEM((2 * PW, PAY), BF),
            pltpu.VMEM((2, len(SPLIT), LANES, COLS), F32),
            pltpu.VMEM((GROUPS, CHIPS_G, NC * CAP, MW), BF),
            pltpu.VMEM((GROUPS, CHIPS_G, NC * CAP, MW), BF),
            pltpu.VMEM((ROWS_G, D), BF),
            pltpu.VMEM((GROUPS, NX, PAY, ROWS_G), BF),
            pltpu.VMEM((GROUPS, PAY, NX * ROWS_G), BF),
            pltpu.VMEM((SPLIT[0] * OWNERS, NX * ROWS_G), BF),
            pltpu.VMEM((4 * LANES, NX * ROWS_G), BF),
            pltpu.VMEM((len(SPLIT), SPLIT[0] * OWNERS, 4 * LANES), F32),
            pltpu.VMEM((NC, CHIPS, 12, LANES), F32),
            pltpu.VMEM((CHIPS, 12, LANES), F32),
            pltpu.VMEM((CHIPS, 12, LANES), F32),
            pltpu.VMEM((CHIPS, 12, LANES), F32),
            dma((9,)),
            dma((4,)),
            dma((4,)),
            dma((GROUPS,)),
            dma((GROUPS,)),
            dma((7,)),
            dma((7,)),
            dma((GROUPS, NX)),
            dma((GROUPS, NX)),
            dma((1,)),
            dma(()),
            dma(()),
            dma(()),
            dma(()),
            dma((GROUPS, NX)),
        ],
        compiler_params=pltpu.CompilerParams(
            collective_id=0, has_side_effects=True, vmem_limit_bytes=56 * 2**20
        ),
    )(
        embeddings,
        coarse_list_index.reshape(1, ROW_DEV),
        slots.reshape(1, ROW_DEV),
        codes,
        centroids,
        rotation.T,
        old_codebook,
        jnp.asarray(spread, BF),
        jnp.asarray(back, F32),
    )
    return store.T, book


def solution(mesh):
    return jax.shard_map(
        shards,
        mesh=mesh,
        in_specs=(
            P(("list", "sub"), None),
            P(("list", "sub")),
            P(("list", "sub")),
            P(("list", "sub"), None),
            P("list", None),
            P(None, "sub"),
            P("list", "sub"),
        ),
        out_specs=(P("list", "sub"), P("list", "sub")),
        check_vma=False,
    )
```

time: 452 us -> 78.7 us (0.17); the launches traced: 447 us -> 78.6 us
  blocking collectives: 264 us -> 0 us
  Pallas kernels: 0 us -> 74.8 us
  waiting for transfers between devices: 68 us -> 0 us
  matrix products: 31.2 us -> 0 us
  other arithmetic: 26.8 us -> 0 us
  starting transfers between devices: 22.7 us -> 0 us
  local copies, waits for them, and re-layouts: 19.2 us -> 3.12 us
  between operations: 14.2 us -> 0.65 us
    psum x1 -> x0, blocking collectives: 246 us -> none  [shards(): total_sums, total_counts = lax.psum((sums, counts), 'list')]
    pallas_call x0 -> x1, Pallas kernels: none -> 74.8 us  [shards(): pl.pallas_call(kernel, out_shape=(jax.ShapeDtypeStruct((COLS, OWNERS * NX...]
    all_to_all x3 -> x0, waiting for transfers between devices: 46 us -> none  [the longest x1 30.6 us: shards(): lax.all_to_all(outbound, 'list', split_axis=0, concat_axis=0, tiled=True)]
    dot_general x9 -> x0, matrix products: 31.2 us -> none  [the longest x8 25.5 us: single_update_step(): jnp.einsum('hme,hmc->mec', indicator_matrix, residual_value_slice, prefer...]
    all_to_all x3 -> x0, starting transfers between devices: 22.7 us -> none  [the longest x1 13.2 us: shards(): lax.all_to_all(local_out, 'list', split_axis=0, concat_axis=0, tiled=True)]
    all_gather x1 -> x0, waiting for transfers between devices: 22 us -> none  [shards(): lax.all_gather(residual, 'sub', axis=0, tiled=True)]
    reduce_sum x8 -> x0, other arithmetic: 21 us -> none  [single_update_step(): part_counts = jnp.sum(indicator_matrix, axis=0, dtype=jnp.float32)]
    all_to_all x1 -> x0, blocking collectives: 18.1 us -> none  [shards(): lax.all_to_all(code_out, 'list', split_axis=0, concat_axis=0, tiled=True)]
  transfers between devices with their start and end apart: 5 -> 0, of which waited for: 4 -> 0; matrix products, arithmetic and copies ran while one was open for 3% -> 0% of each run, Pallas kernels for 0% -> 0%
where the time goes in v1:
time: 78.7 us; the launch traced here: 78.6 us
  Pallas kernels  74.8 us (95%)
  local copies, waits for them, and re-layouts  3.12 us (4%)
    pallas_call x1, Pallas kernels, shards(): pl.pallas_call(kernel, out_shape=(jax.ShapeDtypeStruct((COLS, OWNERS * NX...  74.8 us
    unnamed x4, local copies, waits for them, and re-layouts  3.12 us

profile of v1, /device:TPU:1, one launch (start us, length us, event | category | flops | bytes accessed | tf_op | source)
XLA Modules:
  0.0 78.6 jit_solution(4247108136204218230)
XLA Ops:
  0.6 74.8 %shard_map.104 = (bf16[320,2048]{1,0:T(8,128)(2,1)}, f32[4,320]{1,0:T(4,128)}) custom-call(bf16[256,1280]{1,0:T(8,128)(2,1)} %emb_hbm.1, s32[1,256]{1,0:T(1,128)} %bitcast.6, s32[1,256]{1,0:T(1,128)} %bitcast.7, s32[256,128]{1,0:T(8,128)} %codes_hbm.1, bf16[1024,1280]{1,0:T(8,128)(2,1)} %cent_hbm.1, bf16[320,1280]{1,0:T(8,128)(2,1)} %bitcast.5, ...), custom_call_target="tpu_custom_call" | custom-call | tf_op jit(solution)/shard_map/pallas_call | solution.py:446
  75.4 0.0 copy-start
  75.4 2.5 %copy.13 = bf16[2048,320]{0,1:T(8,128)(2,1)} copy(bf16[2048,320]{0,1:T(8,128)(2,1)} %bitcast.4) | data formatting | bytes 2621440
  78.0 0.0 copy-done
  78.0 0.6 copy.14
Async XLA Ops:
  75.4 2.5 %copy-start = (f32[4,320]{1,0:T(4,128)S(1)}, f32[4,320]{1,0:T(4,128)}, u32[]{:S(2)}) copy-start(f32[4,320]{1,0:T(4,128)} %get-tuple-element.9) | copy-start | bytes 15364

commit v2 on v1

--- a/solution.py
+++ b/solution.py
@@ -24,7 +24,7 @@
 CHIPS_G = 8
 CHIPS = NY * NZ
 ROWS_G = CHIPS_G * NC * CAP
-MW = D + 256
+MW = D + 128
 PW = 384
 PAY = COLS + SUBS_DEV
 NT = (((1,), (1,)), ((), ()))
@@ -75,7 +75,10 @@
     back,
     outb,
     inb,
+    ids_out,
+    ids_in,
     res,
+    code_rows,
     pay_out,
     pay_in,
     hot,
@@ -90,6 +93,8 @@
     swap_recv,
     out_sem,
     in_sem,
+    ids_send,
+    ids_recv,
     rot_send,
     rot_recv,
     pay_send,
@@ -111,10 +116,15 @@
     right, left = lax.rem(x + 1, NX), lax.rem(x + NX - 1, NX)
     across = lax.rem(x + 2, NX)
 
-    sources = [(emb_hbm, emb), (idx_hbm, idx), (slot_hbm, slot), (codes_hbm, codes)]
+    own_rows = pl.ds(pl.multiple_of(core * ROW_DEV, ROW_DEV), ROW_DEV)
+    sources = [
+        (emb_hbm, emb.at[own_rows, 0:D]),
+        (idx_hbm, idx.at[core]),
+        (slot_hbm, slot.at[core]),
+        (codes_hbm, codes.at[own_rows, :]),
+    ]
     loads = [
-        pltpu.make_async_copy(src, dst.at[core], load_sem.at[i])
-        for i, (src, dst) in enumerate(sources)
+        pltpu.make_async_copy(src, dst, load_sem.at[i]) for i, (src, dst) in enumerate(sources)
     ]
     later = [(cent_hbm, cent), (rot_hbm, rot.at[x]), (spread_hbm, spread), (back_hbm, back)]
     later.append((old_hbm, old))
@@ -144,7 +154,7 @@
     swaps = [
         pltpu.make_async_remote_copy(
             src_ref=src,
-            dst_ref=dst.at[core],
+            dst_ref=dst,
             send_sem=swap_send.at[i],
             recv_sem=swap_recv.at[i],
             device_id=(sibling, x),
@@ -179,12 +189,25 @@
         load.wait()
     for swap in swaps:
         swap.wait_recv()
+    emb[:, D:MW] = (codes[...] + 1).astype(F32).astype(BF)
+    keys, uppers, lowers = [], [], []
+    for c in range(NC):
+        list_id = idx[c]
+        owner = list_id // LIST_DEV
+        key = (owner // NC * NC + c) * CAP + slot[c]
+        keys.append(jnp.where(lax.rem(owner, NC) == core, key, -1))
+        local = lax.rem(list_id, LIST_DEV)
+        uppers.append((local // 4 + 1).astype(F32).astype(BF))
+        lowers.append(lax.rem(local, 4).astype(F32).astype(BF))
+    key = jnp.concatenate(keys, axis=1)
+    upper_id = jnp.concatenate(uppers, axis=1)
+    lower_id = jnp.concatenate(lowers, axis=1)
     row_iota = lax.broadcasted_iota(jnp.int32, (ROWS_G, 1), 0)
     lane_iota = lax.broadcasted_iota(jnp.int32, (1, LANES), 1)
 
-    def row_copy(g, j, l):
+    def row_copy(g, l, to_z):
         return pltpu.make_async_remote_copy(
-            src_ref=outb.at[g, j],
+            src_ref=outb.at[g, to_z],
             dst_ref=inb.at[g, z],
             send_sem=out_sem.at[g],
             recv_sem=in_sem.at[g],
@@ -192,43 +215,42 @@
             device_id_type=MESH,
         )
 
+    def ids_copy(g, l):
+        return pltpu.make_async_remote_copy(
+            src_ref=ids_out.at[g],
+            dst_ref=ids_in.at[g, z],
+            send_sem=ids_send.at[g],
+            recv_sem=ids_recv.at[g],
+            device_id=(l, x),
+            device_id_type=MESH,
+        )
+
     def send_group(g, carry):
         to_y = lax.rem(y + g, NY)
-        to_z = lax.rem(z + row_iota // (NC * CAP), NZ)
-        wanted = (to_y * NZ + to_z) * (NC * CAP) + lax.rem(row_iota, NC * CAP)
-        made = jnp.zeros((ROWS_G, D), F32)
-        code_tile = jnp.zeros((ROWS_G, LANES), F32)
-        ids = jnp.zeros((ROWS_G, 1), F32)
-        for c in range(NC):
-            list_id = idx[c]
-            owner = list_id // LIST_DEV
-            target = (owner // NC * NC + c) * CAP + slot[c]
-            match = (wanted == target) & (lax.rem(owner, NC) == core)
-            place = jnp.where(match, 1.0, 0.0).astype(BF)
-            local = lax.rem(list_id, LIST_DEV).astype(F32) + 4.0
-            ids += jnp.sum(jnp.where(match, local, 0.0), axis=1, keepdims=True)
-            code_tile += jnp.dot(
-                place, (codes[c] + 1).astype(F32).astype(BF), preferred_element_type=F32
-            )
-            made += jnp.dot(place, emb[c], preferred_element_type=F32)
-        id_int = ids.astype(jnp.int32)
-        ids_tile = jnp.where(
-            lane_iota < LANES // 2, (id_int // 4).astype(F32), lax.rem(id_int, 4).astype(F32)
-        )
-        outb[g, :, :, 0:D] = made.astype(BF).reshape(CHIPS_G, NC * CAP, D)
-        outb[g, :, :, D : D + LANES] = code_tile.astype(BF).reshape(CHIPS_G, NC * CAP, LANES)
-        outb[g, :, :, D + LANES : MW] = ids_tile.astype(BF).reshape(CHIPS_G, NC * CAP, LANES)
-
-        def send(j, carry):
-            row_copy(g, j, (to_y * NZ + lax.rem(z + j, NZ)) * NC + core).start()
+        place = jnp.where(to_y * ROWS_G + row_iota == key, 1.0, 0.0).astype(BF)
+        ids = 4.0 * lax.dot_general(
+            upper_id, place, NT, preferred_element_type=F32
+        ) + lax.dot_general(lower_id, place, NT, preferred_element_type=F32)
+        ids_out[g] = ids.astype(jnp.int32)
+        made = jnp.dot(place, emb[...], preferred_element_type=F32)
+        outb[g] = made.astype(BF).reshape(CHIPS_G, NC * CAP, MW)
+
+        def send(k, carry):
+            step = jnp.where(lax.rem(k, 2) == 1, (k + 1) // 2, NZ - k // 2)
+            to_z = lax.rem(z + step, NZ)
+            l = (to_y * NZ + to_z) * NC + core
+            ids_copy(g, l).start()
+            row_copy(g, l, to_z).start()
             return carry
 
         lax.fori_loop(jnp.where(g == 0, 1, 0), CHIPS_G, send, 0)
         return carry
 
-    lax.fori_loop(0, GROUPS, send_group, 0)
-    own_block = pltpu.make_async_copy(outb.at[0, 0], inb.at[0, z], own_sem.at[0])
+    send_group(0, 0)
+    own_block = pltpu.make_async_copy(outb.at[0, z], inb.at[0, z], own_sem.at[0])
     own_block.start()
+    ids_in[0, z] = ids_out[0]
+    lax.fori_loop(1, GROUPS, send_group, 0)
 
     def to_sibling(block, number):
         copy = rot_copy(rot.at[block, half_rows, :], block, half_rows, number, sibling, x)
@@ -259,6 +281,9 @@
     same = lax.broadcasted_iota(jnp.int32, (LANES, LANES), 0) == lax.broadcasted_iota(
         jnp.int32, (LANES, LANES), 1
     )
+    lane_of_row = lax.broadcasted_iota(
+        jnp.int32, (CHIPS_G, NC * CAP, LANES), 2
+    ) == z * NC * CAP + lax.broadcasted_iota(jnp.int32, (CHIPS_G, NC * CAP, LANES), 1)
     unit = jnp.where(same, 1.0, 0.0).astype(BF)
 
     def group_copy(g, many):
@@ -267,6 +292,16 @@
             dst_ref=inb.at[g, 0:many],
             send_sem=out_sem.at[g],
             recv_sem=in_sem.at[g],
+            device_id=(sibling, x),
+            device_id_type=MESH,
+        )
+
+    def ids_group_copy(g, many):
+        return pltpu.make_async_remote_copy(
+            src_ref=ids_in.at[g, 0:many],
+            dst_ref=ids_in.at[g, 0:many],
+            send_sem=ids_send.at[g],
+            recv_sem=ids_recv.at[g],
             device_id=(sibling, x),
             device_id_type=MESH,
         )
@@ -295,31 +330,35 @@
         @pl.when(g == 0)
         def _():
             group_copy(0, CHIPS_G - 1).wait_recv()
+            ids_group_copy(0, CHIPS_G - 1).wait_recv()
 
         @pl.when(g > 0)
         def _():
             group_copy(g, CHIPS_G).wait_recv()
-
-        ids_tile = inb[g, :, :, D + LANES : MW].astype(F32).reshape(ROWS_G, LANES)
-        list_row = (
-            ids_tile[:, 0:1] * 4.0 + ids_tile[:, LANES // 2 : LANES // 2 + 1] - 4.0
-        ).astype(jnp.int32)
+            ids_group_copy(g, CHIPS_G).wait_recv()
+
+        ids = jnp.where(lane_of_row, ids_in[g].astype(F32), 0.0)
+        list_row = jnp.sum(ids, axis=2, keepdims=True).reshape(ROWS_G, 1).astype(jnp.int32) - 4
         chosen = jnp.where(list_row == list_iota, 1.0, 0.0).astype(BF)
         for part in range(2):
             cut = slice(part * HALF, (part + 1) * HALF)
             picked = jnp.dot(chosen, cent[:, cut], preferred_element_type=F32)
             rows = inb[g, :, :, cut].astype(F32).reshape(ROWS_G, HALF)
             res[:, cut] = (rows - picked).astype(BF)
-        code_tile = inb[g, :, :, D : D + LANES].reshape(ROWS_G, LANES)
-        code_rows = lax.dot_general(unit, code_tile, NT, preferred_element_type=F32).astype(BF)
-        for t in range(NX):
-            turned = lax.dot_general(rot[t], res[...], NT, preferred_element_type=F32)
-            pay_out[g, t, 0:COLS, :] = turned.astype(BF)
-            pay_out[g, t, COLS:PAY, :] = code_rows[t * SUBS_DEV : (t + 1) * SUBS_DEV, :]
-        for dt in (2, 1, 3):
-            pay_copy(g, dt).start()
+        code_tile = inb[g, :, :, D:MW].reshape(ROWS_G, LANES)
+        code_rows[...] = lax.dot_general(unit, code_tile, NT, preferred_element_type=F32).astype(BF)
         own = pl.ds(pl.multiple_of(x * ROWS_G, ROWS_G), ROWS_G)
-        pay_in[g, :, own] = pay_out[g, x]
+        for dt in (2, 1, 3, 0):
+            t = lax.rem(x + dt, NX)
+            turned = lax.dot_general(rot[t], res[...], NT, preferred_element_type=F32).astype(BF)
+            mine = code_rows[pl.ds(pl.multiple_of(t * SUBS_DEV, SUBS_DEV), SUBS_DEV), :]
+            if dt:
+                pay_out[g, t, 0:COLS, :] = turned
+                pay_out[g, t, COLS:PAY, :] = mine
+                pay_copy(g, dt).start()
+            else:
+                pay_in[g, 0:COLS, own] = turned
+                pay_in[g, COLS:PAY, own] = mine
 
     def count_group(g):
         for dt in range(1, NX):
@@ -424,8 +463,10 @@
     for swap in swaps:
         swap.wait_send()
     group_copy(0, CHIPS_G - 1).wait_send()
+    ids_group_copy(0, CHIPS_G - 1).wait_send()
     for g in range(1, GROUPS):
         group_copy(g, CHIPS_G).wait_send()
+        ids_group_copy(g, CHIPS_G).wait_send()
     for copy in [to_right, to_left, on_right, on_left] + shared:
         copy.wait_send()
     for g in range(GROUPS):
@@ -452,10 +493,10 @@
         in_specs=[anywhere] * 9,
         out_specs=(anywhere, vmem),
         scratch_shapes=[
-            pltpu.VMEM((NC, ROW_DEV, D), BF),
+            pltpu.VMEM((NC * ROW_DEV, MW), BF),
             pltpu.VMEM((NC, 1, ROW_DEV), jnp.int32),
             pltpu.VMEM((NC, 1, ROW_DEV), jnp.int32),
-            pltpu.VMEM((NC, ROW_DEV, LANES), jnp.int32),
+            pltpu.VMEM((NC * ROW_DEV, LANES), jnp.int32),
             pltpu.VMEM((LIST_DEV, D), BF),
             pltpu.VMEM((NX, COLS, D), BF),
             pltpu.VMEM((CENT // OWNERS, COLS), F32),
@@ -463,7 +504,10 @@
             pltpu.VMEM((2, len(SPLIT), LANES, COLS), F32),
             pltpu.VMEM((GROUPS, CHIPS_G, NC * CAP, MW), BF),
             pltpu.VMEM((GROUPS, CHIPS_G, NC * CAP, MW), BF),
+            pltpu.VMEM((GROUPS, 1, LANES), jnp.int32),
+            pltpu.VMEM((GROUPS, CHIPS_G, 1, LANES), jnp.int32),
             pltpu.VMEM((ROWS_G, D), BF),
+            pltpu.VMEM((LANES, ROWS_G), BF),
             pltpu.VMEM((GROUPS, NX, PAY, ROWS_G), BF),
             pltpu.VMEM((GROUPS, PAY, NX * ROWS_G), BF),
             pltpu.VMEM((SPLIT[0] * OWNERS, NX * ROWS_G), BF),
@@ -476,6 +520,8 @@
             dma((9,)),
             dma((4,)),
             dma((4,)),
+            dma((GROUPS,)),
+            dma((GROUPS,)),
             dma((GROUPS,)),
             dma((GROUPS,)),
             dma((7,)),

time: 78.7 us -> 74.9 us (0.952)
  Pallas kernels: 74.8 us -> 71 us
    pallas_call x1, Pallas kernels: 74.8 us -> 71 us  [shards(): pl.pallas_call(kernel, out_shape=(jax.ShapeDtypeStruct((COLS, OWNERS * NX...]
where the time goes in v2:
time: 74.9 us; the launch traced here: 74.8 us
  Pallas kernels  71 us (95%)
  local copies, waits for them, and re-layouts  3.12 us (4%)
    pallas_call x1, Pallas kernels, shards(): pl.pallas_call(kernel, out_shape=(jax.ShapeDtypeStruct((COLS, OWNERS * NX...  71 us
    unnamed x4, local copies, waits for them, and re-layouts  3.12 us

profile of v2, /device:TPU:1, one launch (start us, length us, event | category | flops | bytes accessed | tf_op | source)
XLA Modules:
  0.0 74.8 jit_solution(14396900239119329557)
XLA Ops:
  0.6 71.0 %shard_map.104 = (bf16[320,2048]{1,0:T(8,128)(2,1)}, f32[4,320]{1,0:T(4,128)}) custom-call(bf16[256,1280]{1,0:T(8,128)(2,1)} %emb_hbm.1, s32[1,256]{1,0:T(1,128)} %bitcast.6, s32[1,256]{1,0:T(1,128)} %bitcast.7, s32[256,128]{1,0:T(8,128)} %codes_hbm.1, bf16[1024,1280]{1,0:T(8,128)(2,1)} %cent_hbm.1, bf16[320,1280]{1,0:T(8,128)(2,1)} %bitcast.5, ...), custom_call_target="tpu_custom_call" | custom-call | tf_op jit(solution)/shard_map/pallas_call | solution.py:487
  71.7 0.0 copy-start
  71.7 2.5 %copy.13 = bf16[2048,320]{0,1:T(8,128)(2,1)} copy(bf16[2048,320]{0,1:T(8,128)(2,1)} %bitcast.4) | data formatting | bytes 2621440
  74.2 0.0 copy-done
  74.2 0.6 copy.14
Async XLA Ops:
  71.7 2.5 %copy-start = (f32[4,320]{1,0:T(4,128)S(1)}, f32[4,320]{1,0:T(4,128)}, u32[]{:S(2)}) copy-start(f32[4,320]{1,0:T(4,128)} %get-tuple-element.9) | copy-start | bytes 15364

commit v3 on v2

--- a/solution.py
+++ b/solution.py
@@ -38,7 +38,7 @@
 
 def layout_tables():
     spread = np.zeros((2 * PW, PAY), np.float32)
-    back = np.zeros((2, len(SPLIT), LANES, COLS), np.float32)
+    back = np.zeros((PW, 2 * PW), np.float32)
     for g, (first, many) in enumerate(zip(FIRST, SPLIT)):
         for i in range(many):
             m = first + i
@@ -47,8 +47,8 @@
                 spread[PW + g * LANES + lane, COLS + m] = 1
                 if d < DSUB:
                     spread[g * LANES + lane, m * DSUB + d] = 1
-                    back[0, g, lane, m * DSUB + d] = 1
-                    back[1, g, i * (DSUB + 1) + DSUB, m * DSUB + d] = 1
+                    back[g * LANES + lane, m * DSUB + d] = 1
+                    back[g * LANES + i * (DSUB + 1) + DSUB, PW + m * DSUB + d] = 1
     return spread, back
 
 
@@ -131,7 +131,7 @@
     loads += [
         pltpu.make_async_copy(src, dst, load_sem.at[4 + i]) for i, (src, dst) in enumerate(later)
     ]
-    for load in loads:
+    for load in loads[:4]:
         load.start()
 
     barrier = pltpu.get_barrier_semaphore()
@@ -184,6 +184,8 @@
     to_left = rot_copy(rot_hbm.at[half_rows, :], x, half_rows, 1, me, left)
     to_right.start()
     to_left.start()
+    for load in loads[4:]:
+        load.start()
 
     for load in loads[:4]:
         load.wait()
@@ -236,14 +238,14 @@
         outb[g] = made.astype(BF).reshape(CHIPS_G, NC * CAP, MW)
 
         def send(k, carry):
-            step = jnp.where(lax.rem(k, 2) == 1, (k + 1) // 2, NZ - k // 2)
+            step = NZ // 2 + jnp.where(lax.rem(k, 2) == 1, -((k + 1) // 2), k // 2)
             to_z = lax.rem(z + step, NZ)
             l = (to_y * NZ + to_z) * NC + core
             ids_copy(g, l).start()
             row_copy(g, l, to_z).start()
             return carry
 
-        lax.fori_loop(jnp.where(g == 0, 1, 0), CHIPS_G, send, 0)
+        lax.fori_loop(0, jnp.where(g == 0, CHIPS_G - 1, CHIPS_G), send, 0)
         return carry
 
     send_group(0, 0)
@@ -360,7 +362,9 @@
                 pay_in[g, 0:COLS, own] = turned
                 pay_in[g, COLS:PAY, own] = mine
 
-    def count_group(g):
+    subspace = lane_iota // (DSUB + 1)
+
+    def count_group(g, after):
         for dt in range(1, NX):
             pay_copy(g, dt).wait_recv()
         for s in range(NX):
@@ -386,24 +390,32 @@
             acc[part, 0 : many * OWNERS, :] += lax.dot_general(
                 hot[0 : many * OWNERS, :], vals[...], NT, preferred_element_type=F32
             )
+            after(part, many)
 
     acc[...] = jnp.zeros_like(acc)
 
     def both(g, carry):
-        @pl.when(g < GROUPS)
-        def _():
-            rotate_group(g)
+        rotate_group(g)
 
         @pl.when(g > 0)
         def _():
-            count_group(g - 1)
+            count_group(g - 1, lambda part, many: None)
 
         return carry
 
-    lax.fori_loop(0, GROUPS + 1, both, 0)
-
-    subspace = lane_iota // (DSUB + 1)
-    for part, many in enumerate(SPLIT):
+    lax.fori_loop(0, GROUPS, both, 0)
+
+    def pair_copy(part):
+        return pltpu.make_async_remote_copy(
+            src_ref=sum_out.at[part, 1 - core],
+            dst_ref=sum_pair.at[part],
+            send_sem=pair_send.at[part],
+            recv_sem=pair_recv.at[part],
+            device_id=(sibling, x),
+            device_id_type=MESH,
+        )
+
+    def finish_part(part, many):
         for lo in range(4):
             cut = slice(lo * LANES, (lo + 1) * LANES)
             total = jnp.zeros((OWNERS, LANES), F32)
@@ -411,19 +423,13 @@
                 total = jnp.where(
                     subspace == i, acc[part, i * OWNERS : (i + 1) * OWNERS, cut], total
                 )
-            sum_out[:, :, part * 4 + lo, :] = total.reshape(NC, CHIPS, LANES)
-
-    pair = pltpu.make_async_remote_copy(
-        src_ref=sum_out.at[1 - core],
-        dst_ref=sum_pair,
-        send_sem=pair_send,
-        recv_sem=pair_recv,
-        device_id=(sibling, x),
-        device_id_type=MESH,
-    )
-    pair.start()
-    pair.wait_recv()
-    sum_mid[...] = sum_out[core] + sum_pair[...]
+            sum_out[part, :, :, lo, :] = total.reshape(NC, CHIPS, LANES)
+        pair_copy(part).start()
+
+    count_group(GROUPS - 1, finish_part)
+    for part in range(len(SPLIT)):
+        pair_copy(part).wait_recv()
+        sum_mid[:, part * 4 : part * 4 + 4, :] = sum_out[part, core] + sum_pair[part]
 
     def send_sum(k, carry):
         pltpu.make_async_remote_copy(
@@ -448,16 +454,17 @@
     )
     all_sums.wait_recv()
     total = jnp.sum(sum_in[...], axis=0)
-    sums = jnp.zeros((4, COLS), F32)
-    counts = jnp.zeros((4, COLS), F32)
-    for part in range(len(SPLIT)):
-        tile = total[part * 4 : part * 4 + 4, :]
-        sums += jnp.dot(
-            tile, back[0, part], preferred_element_type=F32, precision=lax.Precision.HIGHEST
-        )
-        counts += jnp.dot(
-            tile, back[1, part], preferred_element_type=F32, precision=lax.Precision.HIGHEST
-        )
+    high = jnp.concatenate([total[part * 4 : part * 4 + 4] for part in range(len(SPLIT))], axis=1)
+    terms = []
+    for _ in range(3):
+        term = high.astype(BF).astype(F32)
+        terms.append(term)
+        high = high - term
+    placed = jnp.dot(
+        jnp.concatenate(terms, axis=0).astype(BF), back[...], preferred_element_type=F32
+    )
+    placed = (placed[8:12] + placed[4:8]) + placed[0:4]
+    sums, counts = placed[:, 0:COLS], placed[:, PW : PW + COLS]
     book_ref[...] = (sums + ANCHOR * old[...]) / (counts + ANCHOR)
 
     for swap in swaps:
@@ -472,7 +479,8 @@
     for g in range(GROUPS):
         for dt in range(1, NX):
             pay_copy(g, dt).wait_send()
-    pair.wait_send()
+    for part in range(len(SPLIT)):
+        pair_copy(part).wait_send()
     all_sums.wait_send()
     for g in range(GROUPS):
         for s in range(NX):
@@ -501,7 +509,7 @@
             pltpu.VMEM((NX, COLS, D), BF),
             pltpu.VMEM((CENT // OWNERS, COLS), F32),
             pltpu.VMEM((2 * PW, PAY), BF),
-            pltpu.VMEM((2, len(SPLIT), LANES, COLS), F32),
+            pltpu.VMEM((PW, 2 * PW), BF),
             pltpu.VMEM((GROUPS, CHIPS_G, NC * CAP, MW), BF),
             pltpu.VMEM((GROUPS, CHIPS_G, NC * CAP, MW), BF),
             pltpu.VMEM((GROUPS, 1, LANES), jnp.int32),
@@ -513,8 +521,8 @@
             pltpu.VMEM((SPLIT[0] * OWNERS, NX * ROWS_G), BF),
             pltpu.VMEM((4 * LANES, NX * ROWS_G), BF),
             pltpu.VMEM((len(SPLIT), SPLIT[0] * OWNERS, 4 * LANES), F32),
-            pltpu.VMEM((NC, CHIPS, 12, LANES), F32),
-            pltpu.VMEM((CHIPS, 12, LANES), F32),
+            pltpu.VMEM((len(SPLIT), NC, CHIPS, 4, LANES), F32),
+            pltpu.VMEM((len(SPLIT), CHIPS, 4, LANES), F32),
             pltpu.VMEM((CHIPS, 12, LANES), F32),
             pltpu.VMEM((CHIPS, 12, LANES), F32),
             dma((9,)),
@@ -529,8 +537,8 @@
             dma((GROUPS, NX)),
             dma((GROUPS, NX)),
             dma((1,)),
-            dma(()),
-            dma(()),
+            dma((len(SPLIT),)),
+            dma((len(SPLIT),)),
             dma(()),
             dma(()),
             dma((GROUPS, NX)),
@@ -547,7 +555,7 @@
         rotation.T,
         old_codebook,
         jnp.asarray(spread, BF),
-        jnp.asarray(back, F32),
+        jnp.asarray(back, BF),
     )
     return store.T, book
 

time: 74.9 us -> 73.5 us (0.981)
  Pallas kernels: 71 us -> 69.7 us
    pallas_call x1, Pallas kernels: 71 us -> 69.7 us  [shards(): pl.pallas_call(kernel, out_shape=(jax.ShapeDtypeStruct((COLS, OWNERS * NX...]
where the time goes in v3:
time: 73.5 us; the launch traced here: 73.4 us
  Pallas kernels  69.7 us (95%)
  local copies, waits for them, and re-layouts  3.12 us (4%)
    pallas_call x1, Pallas kernels, shards(): pl.pallas_call(kernel, out_shape=(jax.ShapeDtypeStruct((COLS, OWNERS * NX...  69.7 us
    unnamed x4, local copies, waits for them, and re-layouts  3.12 us

profile of v3, /device:TPU:1, one launch (start us, length us, event | category | flops | bytes accessed | tf_op | source)
XLA Modules:
  0.0 73.4 jit_solution(13426233676882488504)
XLA Ops:
  0.6 69.7 %shard_map.104 = (bf16[320,2048]{1,0:T(8,128)(2,1)}, f32[4,320]{1,0:T(4,128)}) custom-call(bf16[256,1280]{1,0:T(8,128)(2,1)} %emb_hbm.1, s32[1,256]{1,0:T(1,128)} %bitcast.6, s32[1,256]{1,0:T(1,128)} %bitcast.7, s32[256,128]{1,0:T(8,128)} %codes_hbm.1, bf16[1024,1280]{1,0:T(8,128)(2,1)} %cent_hbm.1, bf16[320,1280]{1,0:T(8,128)(2,1)} %bitcast.5, ...), custom_call_target="tpu_custom_call" | custom-call | tf_op jit(solution)/shard_map/pallas_call | solution.py:495
  70.3 0.0 copy-start
  70.3 2.5 %copy.13 = bf16[2048,320]{0,1:T(8,128)(2,1)} copy(bf16[2048,320]{0,1:T(8,128)(2,1)} %bitcast.4) | data formatting | bytes 2621440
  72.8 0.0 copy-done
  72.8 0.6 copy.14
Async XLA Ops:
  70.3 2.5 %copy-start = (f32[4,320]{1,0:T(4,128)S(1)}, f32[4,320]{1,0:T(4,128)}, u32[]{:S(2)}) copy-start(f32[4,320]{1,0:T(4,128)} %get-tuple-element.9) | copy-start | bytes 15364

commit v4 on v3

--- a/solution.py
+++ b/solution.py
@@ -21,6 +21,7 @@
 SUBS_DEV = 32
 DSUB = 10
 GROUPS = 4
+LAST = GROUPS - 1
 CHIPS_G = 8
 CHIPS = NY * NZ
 ROWS_G = CHIPS_G * NC * CAP
@@ -227,8 +228,11 @@
             device_id_type=MESH,
         )
 
+    def far_first(k):
+        return NZ // 2 + jnp.where(lax.rem(k, 2) == 1, -((k + 1) // 2), k // 2)
+
     def send_group(g, carry):
-        to_y = lax.rem(y + g, NY)
+        to_y = lax.rem(y + g + 1, NY)
         place = jnp.where(to_y * ROWS_G + row_iota == key, 1.0, 0.0).astype(BF)
         ids = 4.0 * lax.dot_general(
             upper_id, place, NT, preferred_element_type=F32
@@ -238,21 +242,19 @@
         outb[g] = made.astype(BF).reshape(CHIPS_G, NC * CAP, MW)
 
         def send(k, carry):
-            step = NZ // 2 + jnp.where(lax.rem(k, 2) == 1, -((k + 1) // 2), k // 2)
-            to_z = lax.rem(z + step, NZ)
+            to_z = lax.rem(z + far_first(k), NZ)
             l = (to_y * NZ + to_z) * NC + core
             ids_copy(g, l).start()
             row_copy(g, l, to_z).start()
             return carry
 
-        lax.fori_loop(0, jnp.where(g == 0, CHIPS_G - 1, CHIPS_G), send, 0)
+        lax.fori_loop(0, jnp.where(g == LAST, CHIPS_G - 1, CHIPS_G), send, 0)
         return carry
 
-    send_group(0, 0)
-    own_block = pltpu.make_async_copy(outb.at[0, z], inb.at[0, z], own_sem.at[0])
+    lax.fori_loop(0, GROUPS, send_group, 0)
+    own_block = pltpu.make_async_copy(outb.at[LAST, z], inb.at[LAST, z], own_sem.at[0])
     own_block.start()
-    ids_in[0, z] = ids_out[0]
-    lax.fori_loop(1, GROUPS, send_group, 0)
+    ids_in[LAST, z] = ids_out[LAST]
 
     def to_sibling(block, number):
         copy = rot_copy(rot.at[block, half_rows, :], block, half_rows, number, sibling, x)
@@ -320,7 +322,7 @@
         )
 
     def store_copy(g, s):
-        from_y = lax.rem(y - g + NY, NY)
+        from_y = lax.rem(y - g + NY - 1, NY)
         to = pl.multiple_of(s * (OWNERS * CAP) + from_y * ROWS_G, ROWS_G)
         return pltpu.make_async_copy(
             pay_in.at[g, 0:COLS, s * ROWS_G : (s + 1) * ROWS_G],
@@ -329,12 +331,12 @@
         )
 
     def rotate_group(g):
-        @pl.when(g == 0)
+        @pl.when(g == LAST)
         def _():
-            group_copy(0, CHIPS_G - 1).wait_recv()
-            ids_group_copy(0, CHIPS_G - 1).wait_recv()
-
-        @pl.when(g > 0)
+            group_copy(LAST, CHIPS_G - 1).wait_recv()
+            ids_group_copy(LAST, CHIPS_G - 1).wait_recv()
+
+        @pl.when(g < LAST)
         def _():
             group_copy(g, CHIPS_G).wait_recv()
             ids_group_copy(g, CHIPS_G).wait_recv()
@@ -432,21 +434,22 @@
         sum_mid[:, part * 4 : part * 4 + 4, :] = sum_out[part, core] + sum_pair[part]
 
     def send_sum(k, carry):
+        to = lax.rem(y + k // NZ + 1, NY) * NZ + lax.rem(z + far_first(lax.rem(k, NZ)), NZ)
         pltpu.make_async_remote_copy(
-            src_ref=sum_mid.at[lax.rem(chip + k, CHIPS)],
+            src_ref=sum_mid.at[to],
             dst_ref=sum_in.at[k],
             send_sem=sum_send,
             recv_sem=sum_recv,
-            device_id=(peer_of(k), x),
+            device_id=(to * NC + core, x),
             device_id_type=MESH,
         ).start()
         return carry
 
-    lax.fori_loop(1, CHIPS, send_sum, 0)
-    sum_in[0] = sum_mid[chip]
+    lax.fori_loop(0, CHIPS - 1, send_sum, 0)
+    sum_in[CHIPS - 1] = sum_mid[chip]
     all_sums = pltpu.make_async_remote_copy(
-        src_ref=sum_mid.at[1:CHIPS],
-        dst_ref=sum_in.at[1:CHIPS],
+        src_ref=sum_mid.at[0 : CHIPS - 1],
+        dst_ref=sum_in.at[0 : CHIPS - 1],
         send_sem=sum_send,
         recv_sem=sum_recv,
         device_id=(sibling, x),
@@ -469,9 +472,9 @@
 
     for swap in swaps:
         swap.wait_send()
-    group_copy(0, CHIPS_G - 1).wait_send()
-    ids_group_copy(0, CHIPS_G - 1).wait_send()
-    for g in range(1, GROUPS):
+    group_copy(LAST, CHIPS_G - 1).wait_send()
+    ids_group_copy(LAST, CHIPS_G - 1).wait_send()
+    for g in range(LAST):
         group_copy(g, CHIPS_G).wait_send()
         ids_group_copy(g, CHIPS_G).wait_send()
     for copy in [to_right, to_left, on_right, on_left] + shared:

time: 73.5 us -> 72.9 us (level)
  no operation moved by 1% of the time
where the time goes in v4:
time: 72.9 us; the launch traced here: 72.8 us
  Pallas kernels  69 us (95%)
  local copies, waits for them, and re-layouts  3.12 us (4%)
    pallas_call x1, Pallas kernels, shards(): pl.pallas_call(kernel, out_shape=(jax.ShapeDtypeStruct((COLS, OWNERS * NX...  69 us
    unnamed x4, local copies, waits for them, and re-layouts  3.12 us

profile of v4, /device:TPU:1, one launch (start us, length us, event | category | flops | bytes accessed | tf_op | source)
XLA Modules:
  0.0 72.8 jit_solution(4646201158903214301)
XLA Ops:
  0.6 69.0 %shard_map.104 = (bf16[320,2048]{1,0:T(8,128)(2,1)}, f32[4,320]{1,0:T(4,128)}) custom-call(bf16[256,1280]{1,0:T(8,128)(2,1)} %emb_hbm.1, s32[1,256]{1,0:T(1,128)} %bitcast.6, s32[1,256]{1,0:T(1,128)} %bitcast.7, s32[256,128]{1,0:T(8,128)} %codes_hbm.1, bf16[1024,1280]{1,0:T(8,128)(2,1)} %cent_hbm.1, bf16[320,1280]{1,0:T(8,128)(2,1)} %bitcast.5, ...), custom_call_target="tpu_custom_call" | custom-call | tf_op jit(solution)/shard_map/pallas_call | solution.py:498
  69.7 0.0 copy-start
  69.7 2.5 %copy.13 = bf16[2048,320]{0,1:T(8,128)(2,1)} copy(bf16[2048,320]{0,1:T(8,128)(2,1)} %bitcast.4) | data formatting | bytes 2621440
  72.2 0.0 copy-done
  72.2 0.6 copy.14
Async XLA Ops:
  69.7 2.5 %copy-start = (f32[4,320]{1,0:T(4,128)S(1)}, f32[4,320]{1,0:T(4,128)}, u32[]{:S(2)}) copy-start(f32[4,320]{1,0:T(4,128)} %get-tuple-element.9) | copy-start | bytes 15364

commit v5 on v4

--- a/solution.py
+++ b/solution.py
@@ -234,18 +234,18 @@
     def send_group(g, carry):
         to_y = lax.rem(y + g + 1, NY)
         place = jnp.where(to_y * ROWS_G + row_iota == key, 1.0, 0.0).astype(BF)
+        made = jnp.dot(place, emb[...], preferred_element_type=F32)
+        outb[g] = made.astype(BF).reshape(CHIPS_G, NC * CAP, MW)
         ids = 4.0 * lax.dot_general(
             upper_id, place, NT, preferred_element_type=F32
         ) + lax.dot_general(lower_id, place, NT, preferred_element_type=F32)
         ids_out[g] = ids.astype(jnp.int32)
-        made = jnp.dot(place, emb[...], preferred_element_type=F32)
-        outb[g] = made.astype(BF).reshape(CHIPS_G, NC * CAP, MW)
 
         def send(k, carry):
             to_z = lax.rem(z + far_first(k), NZ)
             l = (to_y * NZ + to_z) * NC + core
+            row_copy(g, l, to_z).start()
             ids_copy(g, l).start()
-            row_copy(g, l, to_z).start()
             return carry
 
         lax.fori_loop(0, jnp.where(g == LAST, CHIPS_G - 1, CHIPS_G), send, 0)

time: 72.9 us -> 73 us (level)
  no operation moved by 1% of the time
where the time goes in v5:
time: 73 us; the launch traced here: 72.9 us
  Pallas kernels  69.1 us (95%)
  local copies, waits for them, and re-layouts  3.12 us (4%)
    pallas_call x1, Pallas kernels, shards(): pl.pallas_call(kernel, out_shape=(jax.ShapeDtypeStruct((COLS, OWNERS * NX...  69.1 us
    unnamed x4, local copies, waits for them, and re-layouts  3.12 us

profile of v5, /device:TPU:1, one launch (start us, length us, event | category | flops | bytes accessed | tf_op | source)
XLA Modules:
  0.0 72.9 jit_solution(10020537335602471459)
XLA Ops:
  0.6 69.1 %shard_map.104 = (bf16[320,2048]{1,0:T(8,128)(2,1)}, f32[4,320]{1,0:T(4,128)}) custom-call(bf16[256,1280]{1,0:T(8,128)(2,1)} %emb_hbm.1, s32[1,256]{1,0:T(1,128)} %bitcast.6, s32[1,256]{1,0:T(1,128)} %bitcast.7, s32[256,128]{1,0:T(8,128)} %codes_hbm.1, bf16[1024,1280]{1,0:T(8,128)(2,1)} %cent_hbm.1, bf16[320,1280]{1,0:T(8,128)(2,1)} %bitcast.5, ...), custom_call_target="tpu_custom_call" | custom-call | tf_op jit(solution)/shard_map/pallas_call | solution.py:498
  69.7 0.0 copy-start
  69.8 2.5 %copy.13 = bf16[2048,320]{0,1:T(8,128)(2,1)} copy(bf16[2048,320]{0,1:T(8,128)(2,1)} %bitcast.4) | data formatting | bytes 2621440
  72.3 0.0 copy-done
  72.3 0.6 copy.14
Async XLA Ops:
  69.7 2.5 %copy-start = (f32[4,320]{1,0:T(4,128)S(1)}, f32[4,320]{1,0:T(4,128)}, u32[]{:S(2)}) copy-start(f32[4,320]{1,0:T(4,128)} %get-tuple-element.9) | copy-start | bytes 15364
